TPU v7x, 512 devices: a whole 4x8x8 slice. The times are simulated.
512 devices in a mesh: lat: 8 (over z_lo, core), lon: 64 (over z_hi, x, y).
Axes of the slice: x: 4, y: 8, z: 8 (z_hi: 2, z_lo: 4; z = z_hi * 4 + z_lo), core: 2. Of those that a mesh axis runs over, the one named last changes fastest.
Arguments:
- background_state: bfloat16 [18, 5760, 1024], P(None, 'lon', 'lat'), may hold values from -6 to 6
- perturbation: bfloat16 [18, 5760, 1024], P(None, 'lon', 'lat'), may hold values from -16 to 16
- surface_pattern_index: int32 [5760, 1024], P('lon', 'lat'), may hold values from 0 to 15
- surface_amplitude_table: float32 [16], replicated, may hold values from -4 to 4
- cutoff: int32 [1024], P('lat'), may hold values from 4 to 64, as said below
- zonal_row_weight: float32 [1024], P('lat'), may hold values from 0.5 to 2
- diffusivity: float32 [18], replicated, may hold values from 0.04 to 0.25
- input_weight: bfloat16 [48, 18], replicated, may hold values from -1.5 to 1.5
- bias: float32 [48], replicated, may hold values from -4 to 4
- output_weight: float32 [18, 48], replicated, may hold values from -0.875 to 0.875
Outputs:
- tangent: bfloat16 [18, 5760, 1024], P(None, 'lon', 'lat')
- gradient: bfloat16 [18, 5760, 1024], P(None, 'lon', 'lat')
Inputs may be any that keep to these rules, and one draw needn't show every extreme that they name: Rows 64 or more rows away from both ends of the grid have cutoff 64; the first and last rows have cutoff 4; a row d < 64 rows from the nearer end has cutoff at least 4 + (d * 60) // 64.
All inputs are finite; a program needn't handle non-finite values.
Results may differ from a plain program's by a relative error of at most 0.001.
Values sent between devices are 32-bit elements; how exact they have to be, the bound alone decides.
A program may use at most 64 MiB of HBM per device.

v0:
```python
import math

import jax
import jax.numpy as jnp
from jax import lax
from jax.sharding import PartitionSpec as P

LONGITUDE_COUNT = 5760
KW = 64
POLAR = 64


TOP_PRECISION = lax.Precision.HIGHEST


def padded(x, sides, width, wrap):
    for axis, dim in sides:
        count, length = (lax.axis_size(axis), x.shape[dim])
        up = [(i, (i + 1) % count) for i in range(count if wrap else count - 1)]
        down = [(j, i) for i, j in up]
        last = lax.slice_in_dim(x, length - width, length, axis=dim)
        leading = lax.slice_in_dim(x, 0, width, axis=dim)
        before = lax.ppermute(last, axis, up)
        after = lax.ppermute(leading, axis, down)
        x = jnp.concatenate([before, x, after], axis=dim)
    return x


def spectral_table(longitudes):
    wave_numbers = jnp.arange(1, KW + 1, dtype=jnp.int32)
    phase_index = longitudes[:, None] * wave_numbers[None, :] % LONGITUDE_COUNT
    angles = phase_index.astype(jnp.float32) * (2.0 * math.pi / LONGITUDE_COUNT)
    return jnp.concatenate([jnp.cos(angles), jnp.sin(angles)], axis=1)


def removal_weights(cutoff):
    wave_numbers = jnp.arange(1, KW + 1, dtype=jnp.float32)[:, None]
    cut_limit = cutoff.astype(jnp.float32)[None, :]
    cut_ratio = cut_limit / wave_numbers
    damping = jnp.where(wave_numbers > cut_limit, 1.0 - cut_ratio * cut_ratio, 0.0)
    return jnp.concatenate([damping, damping], axis=0)


def analyze(state_grid_field, fourier_basis_table):
    return jnp.einsum("hpu,pa->hau", state_grid_field, fourier_basis_table, precision=TOP_PRECISION)


def rebuild(fourier_spectra, fourier_basis_table):
    return jnp.einsum(
        "zum,gu->zgm", fourier_spectra, fourier_basis_table, precision=TOP_PRECISION
    ) * (2.0 / LONGITUDE_COUNT)


def diffuse(state_grid_field, diffusivity, zonal_row_weight):
    cycle_padded = padded(state_grid_field, (("lon", 1),), 1, True)
    band_padded = padded(state_grid_field, (("lat", 2),), 1, False)
    zonal_term = cycle_padded[:, 2:, :] + cycle_padded[:, :-2, :] - 2.0 * state_grid_field
    meridional = band_padded[:, :, 2:] + band_padded[:, :, :-2] - 2.0 * state_grid_field
    return diffusivity[:, None, None] * (zonal_row_weight[None, None, :] * zonal_term + meridional)


def summed_spectra(polar_slab, fourier_basis_table):
    local_spectra = analyze(polar_slab, fourier_basis_table)
    return lax.psum(local_spectra, "lon")


def cycle_filter(polar_slab, weight_set, fourier_basis_table):
    fourier_spectra = summed_spectra(polar_slab, fourier_basis_table)
    filtered = polar_slab - rebuild(fourier_spectra * weight_set[None], fourier_basis_table)
    return (filtered,)


def per_device(
    background_state,
    perturbation,
    surface_pattern_index,
    surface_amplitude_table,
    cutoff,
    zonal_row_weight,
    diffusivity,
    input_weight,
    bias,
    output_weight,
):
    lon_dev = background_state.shape[1]
    lat_dev = background_state.shape[2]
    pattern_values = jnp.arange(surface_amplitude_table.shape[0], dtype=jnp.int32)
    surface_field = jnp.sum(
        jnp.where(
            surface_pattern_index[None] == pattern_values[:, None, None],
            surface_amplitude_table[:, None, None],
            0.0,
        ),
        axis=0,
    )
    start_pert = perturbation.astype(jnp.float32)
    perturbation_field = jnp.concatenate(
        [start_pert[:1] + surface_field[None], start_pert[1:]], axis=0
    )
    before_activation = (
        jnp.einsum(
            "vb,bqf->vqf", input_weight, background_state, preferred_element_type=jnp.float32
        )
        + bias[:, None, None]
    )
    active = jnp.tanh(before_activation)
    activation_slope = 1.0 - active * active
    wide_weight = input_weight.astype(jnp.float32)
    hidden_forward = (
        jnp.einsum("vb,bqf->vqf", wide_weight, perturbation_field, precision=TOP_PRECISION)
        * activation_slope
    )
    tangent_image = (
        perturbation_field
        + diffuse(perturbation_field, diffusivity, zonal_row_weight)
        + 0.5 * jnp.einsum("sm,mxq->sxq", output_weight, hidden_forward, precision=TOP_PRECISION)
    )
    last_band = lax.axis_index("lat") == lax.axis_size("lat") - 1

    def orient(values_in):
        return jnp.where(last_band, jnp.flip(values_in, axis=-1), values_in)

    slab_start = jnp.where(last_band, lat_dev - POLAR, 0).astype(jnp.int32)
    polar_cut = orient(lax.dynamic_slice_in_dim(cutoff, slab_start, POLAR, 0))
    weight_set = removal_weights(polar_cut)
    longitudes = lax.axis_index("lon") * lon_dev + jnp.arange(lon_dev, dtype=jnp.int32)
    fourier_basis_table = spectral_table(longitudes)

    def spectral(polar_slab):
        return cycle_filter(polar_slab, weight_set, fourier_basis_table)

    polar_slab = orient(lax.dynamic_slice_in_dim(tangent_image, slab_start, POLAR, 2))
    filtered = spectral(polar_slab)[0]
    tangent_full = lax.dynamic_update_slice_in_dim(tangent_image, orient(filtered), slab_start, 2)
    twice = spectral(orient(lax.dynamic_slice_in_dim(tangent_full, slab_start, POLAR, 2)))[0]
    adjoint_input = lax.dynamic_update_slice_in_dim(tangent_full, orient(twice), slab_start, 2)
    hidden_backward = (
        jnp.einsum("xf,xbe->fbe", output_weight, adjoint_input, precision=TOP_PRECISION)
        * activation_slope
    )
    gradient = (
        adjoint_input
        + diffuse(adjoint_input, diffusivity, zonal_row_weight)
        + 0.5 * jnp.einsum("zo,zmf->omf", wide_weight, hidden_backward, precision=TOP_PRECISION)
    )
    return (tangent_full.astype(jnp.bfloat16), gradient.astype(jnp.bfloat16))


def solution(mesh):
    placed = (
        P(None, "lon", "lat"),
        P(None, "lon", "lat"),
        P("lon", "lat"),
        P(),
        P("lat"),
        P("lat"),
        P(),
        P(),
        P(),
        P(),
    )
    return jax.shard_map(
        per_device,
        mesh=mesh,
        in_specs=placed,
        out_specs=(P(None, "lon", "lat"), P(None, "lon", "lat")),
        check_vma=False,
    )
```

profile of v0, /device:TPU:1, one launch (start us, length us, event | category | flops | bytes accessed | tf_op | source)
XLA Modules:
  0.0 1695.8 jit_solution(2790603785789324412)
XLA Ops:
  7.2 1.4 copy.57
  11.9 1.5 fusion.2
  13.4 1.6 copy.59
  15.0 16.6 collective-permute-start
  31.9 1.9 collective-permute-start.1
  33.9 2.9 collective-permute-start.2
  36.8 3.0 collective-permute-start.3
  39.9 1.5 copy.63
  41.4 3.7 fusion.45
  45.1 1.9 fusion.27
  47.3 4.0 fusion.1
  51.4 1.5 copy.65
  52.9 1.4 copy.60
  54.3 1.4 copy.62
  55.8 3.2 fusion.19
  59.6 1.4 fusion.52
  61.7 762.4 %all-reduce.3.cloned.1.call-done = f32[18,128,64]{1,2,0:T(8,128)} async-done(((f32[18,128,64]{1,2,0:T(8,128)}), f32[18,128,64]{1,2,0:T(8,128)}) %all-reduce.3.cloned.1.call-update) | async-done | bytes 589840 | tf_op jit(solution)/shard_map/psum | solution.py:64
  827.0 1.4 fusion.54
  829.7 789.7 %all-reduce.5.cloned.1.call-done = f32[18,128,64]{1,2,0:T(8,128)} async-done(((f32[18,128,64]{1,2,0:T(8,128)}), f32[18,128,64]{1,2,0:T(8,128)}) %all-reduce.5.cloned.1.call-update) | async-done | bytes 589840 | tf_op jit(solution)/shard_map/psum | solution.py:64
  1621.7 1.5 copy.70
  1623.2 1.5 fusion.50
  1624.7 3.3 fusion.38
  1628.0 1.6 copy.66
  1629.6 9.5 collective-permute-start.4
  1639.5 1.9 collective-permute-start.5
  1641.4 32.0 %collective-permute-start.6 = (f32[18,90,1]{1,2,0:T(1,128)S(1)}, f32[18,90,1]{1,2,0:T(1,128)S(1)}, u32[]{:S(2)}, u32[]{:S(2)}) collective-permute-start(f32[18,90,1]{1,2,0:T(1,128)S(1)} %get-tuple-element.14), channel_id=1, source_target_pairs={{64,0},{128,64},{192,128},{256,192},{320,256},{384,320},{448,384},... | collective-permute-start | bytes 19448 | tf_op jit(solution)/shard_map/ppermute | solution.py:24
  1673.4 2.3 collective-permute-start.7
  1675.7 4.6 fusion
  1680.3 1.6 copy.71
  1682.0 1.4 copy.67
  1683.4 1.5 copy.69
  1684.8 3.0 fusion.10
  (71 shorter events, 13.1 us)
Async XLA Ops:
  7.2 37.9 %copy-start = (bf16[18,90,128]{2,1,0:T(8,128)(2,1)S(1)}, bf16[18,90,128]{2,1,0:T(8,128)(2,1)}, u32[]{:S(2)}) copy-start(bf16[18,90,128]{2,1,0:T(8,128)(2,1)} %param.10) | copy-start | bytes 1244164
  7.2 817.0 %all-reduce.3.cloned.1.call-start = ((), (), s32[]{:S(2)}) async-start(), calls=%async_computation | async-start | bytes 1179648 | tf_op jit(solution)/shard_map/psum | solution.py:64
  9.8 0.8 copy-start.4
  9.8 0.8 copy-start.8
  15.0 37.9 %collective-permute-start = (f32[18,1,128]{2,1,0:T(1,128)S(1)}, f32[18,1,128]{2,1,0:T(1,128)S(1)}, u32[]{:S(2)}, u32[]{:S(2)}) collective-permute-start(f32[18,1,128]{2,1,0:T(1,128)S(1)} %copy.59), channel_id=1, source_target_pairs={{1,0},{2,1},{3,2},{4,3},{5,4},{6,5},{7,6},{8,7},{9,8},{10,9},{11,1... | collective-permute-start | bytes 27656 | tf_op jit(solution)/shard_map/ppermute | solution.py:24
  31.9 22.4 %collective-permute-start.1 = (f32[18,1,128]{2,1,0:T(1,128)S(1)}, f32[18,1,128]{2,1,0:T(1,128)S(1)}, u32[]{:S(2)}, u32[]{:S(2)}) collective-permute-start(f32[18,1,128]{2,1,0:T(1,128)S(1)} %copy.61), channel_id=1, source_target_pairs={{0,1},{1,2},{2,3},{3,4},{4,5},{5,6},{6,7},{7,8},{8,9},{9,10},{10,1... | collective-permute-start | bytes 27656 | tf_op jit(solution)/shard_map/ppermute | solution.py:23
  33.9 21.9 %collective-permute-start.2 = (f32[18,90,1]{1,2,0:T(1,128)S(1)}, f32[18,90,1]{1,2,0:T(1,128)S(1)}, u32[]{:S(2)}, u32[]{:S(2)}) collective-permute-start(f32[18,90,1]{1,2,0:T(1,128)S(1)} %get-tuple-element.18), channel_id=1, source_target_pairs={{64,0},{128,64},{192,128},{256,192},{320,256},{384,320},{448,384},... | collective-permute-start | bytes 19448 | tf_op jit(solution)/shard_map/ppermute | solution.py:24
  36.8 19.0 %collective-permute-start.3 = (f32[18,90,1]{1,2,0:T(1,128)S(1)}, f32[18,90,1]{1,2,0:T(1,128)S(1)}, u32[]{:S(2)}, u32[]{:S(2)}) collective-permute-start(f32[18,90,1]{1,2,0:T(1,128)S(1)} %get-tuple-element.19), channel_id=1, source_target_pairs={{0,64},{64,128},{128,192},{192,256},{256,320},{320,384},{384,448},... | collective-permute-start | bytes 19448 | tf_op jit(solution)/shard_map/ppermute | solution.py:23
  39.9 1.5 copy-start.2
  45.1 2.2 copy-start.3
  45.1 2.2 copy-start.5
  52.9 2.9 copy-start.6
  52.9 2.9 copy-start.7
  59.6 1.7 copy-start.9
  61.1 1558.3 %all-reduce.5.cloned.1.call-start = ((), (), s32[]{:S(2)}) async-start(), calls=%async_computation.1 | async-start | bytes 1179648 | tf_op jit(solution)/shard_map/psum | solution.py:64
  1623.2 1.5 copy-start.1
  1629.6 52.4 %collective-permute-start.4 = (f32[18,1,128]{2,1,0:T(1,128)S(1)}, f32[18,1,128]{2,1,0:T(1,128)S(1)}, u32[]{:S(2)}, u32[]{:S(2)}) collective-permute-start(f32[18,1,128]{2,1,0:T(1,128)S(1)} %copy.66), channel_id=1, source_target_pairs={{1,0},{2,1},{3,2},{4,3},{5,4},{6,5},{7,6},{8,7},{9,8},{10,9},{11,1... | collective-permute-start | bytes 27656 | tf_op jit(solution)/shard_map/ppermute | solution.py:24
  1639.5 43.9 %collective-permute-start.5 = (f32[18,1,128]{2,1,0:T(1,128)S(1)}, f32[18,1,128]{2,1,0:T(1,128)S(1)}, u32[]{:S(2)}, u32[]{:S(2)}) collective-permute-start(f32[18,1,128]{2,1,0:T(1,128)S(1)} %copy.68), channel_id=1, source_target_pairs={{0,1},{1,2},{2,3},{3,4},{4,5},{5,6},{6,7},{7,8},{8,9},{9,10},{10,1... | collective-permute-start | bytes 27656 | tf_op jit(solution)/shard_map/ppermute | solution.py:23
  1641.4 43.4 %collective-permute-start.6 = (f32[18,90,1]{1,2,0:T(1,128)S(1)}, f32[18,90,1]{1,2,0:T(1,128)S(1)}, u32[]{:S(2)}, u32[]{:S(2)}) collective-permute-start(f32[18,90,1]{1,2,0:T(1,128)S(1)} %get-tuple-element.14), channel_id=1, source_target_pairs={{64,0},{128,64},{192,128},{256,192},{320,256},{384,320},{448,384},... | collective-permute-start | bytes 19448 | tf_op jit(solution)/shard_map/ppermute | solution.py:24
  1673.4 11.4 collective-permute-start.7
Sparse Core Ops, SparseCore 0:
  61.2 762.9 all-reduce.2
  828.6 790.6 all-reduce.4
where the time goes:
time: 1700 us
  waiting for transfers between devices  1550 us (91%)
  starting transfers between devices  70.3 us (4%)
  local copies, waits for them, and re-layouts  23.7 us (1%)
  matrix products  21.6 us (1%)
    psum x2, waiting for transfers between devices, summed_spectra(): return lax.psum(local_spectra, 'lon')  1550 us
    ppermute x4, starting transfers between devices, padded(): after = lax.ppermute(leading, axis, down)  61 us
  transfers between devices with their start and end apart: 10, of which 2 were waited for; matrix products, arithmetic and copies ran while one was open for 2% of the time, Pallas kernels for 0%

commit v1 on v0

v1 whole, which is shorter than its diff:
```python
import functools
import math

import jax
import jax.numpy as jnp
import numpy as np
from jax import lax
from jax.experimental import pallas as pl
from jax.experimental.pallas import tpu as pltpu
from jax.sharding import PartitionSpec as P

LONGITUDE_COUNT = 5760
C = 18
HID = 48
L = 90
LP = 96
R = 128
KW = 64
N_LON = 64
N_LAT = 8
F32 = jnp.float32
BF16 = jnp.bfloat16
MESH = pl.DeviceIdType.MESH

WIDTH = [min(64, -(-(8 * a + 4) * 16 // 15)) for a in range(8)]
FOLD = []
for kind in (0, 1):
    FOLD += [((kind, 7), None), ((kind, 6), (kind, 0)), ((kind, 5), (kind, 1)), ((kind, 4), (kind, 2))]
FOLD.append(((0, 3), (1, 3)))
PAIRS = C // 2
PER_OWNER = 2
TILES = PAIRS * len(FOLD)
OWNERS = -(-TILES // PER_OWNER)
SLOTS = OWNERS * PER_OWNER


def base_tables():
    wave = np.arange(1, KW + 1)
    rows = np.zeros((2, LP, 2 * KW), np.float64)
    for row in range(LP):
        if row <= L or row == LP - 1:
            angle = 2 * math.pi * (((row if row <= L else -1) * wave) % LONGITUDE_COUNT) / LONGITUDE_COUNT
            rows[0, row] = np.concatenate([np.cos(angle)] * 2)
            rows[1, row] = np.concatenate([np.sin(angle)] * 2)
    turn = np.zeros((N_LON, 2, 2 * KW), np.float64)
    for p in range(N_LON):
        angle = 2 * math.pi * ((p * L * wave) % LONGITUDE_COUNT) / LONGITUDE_COUNT
        turn[p, 0] = np.concatenate([np.cos(angle), np.sin(angle)])
        turn[p, 1] = np.concatenate([-np.sin(angle), np.cos(angle)])
    return rows.astype(np.float32), turn.astype(np.float32)


def iota(shape, dim):
    return lax.broadcasted_iota(jnp.int32, shape, dim)


def one_hot(mask):
    return jnp.where(mask, 1.0, 0.0).astype(BF16)


def dot(a, b):
    return lax.dot_general(a, b, (((1,), (0,)), ((), ())), preferred_element_type=F32)


def dot_nt(a, b, precision=None):
    return lax.dot_general(a, b, (((1,), (1,)), ((), ())), preferred_element_type=F32, precision=precision)


def split(x):
    high = x.astype(BF16)
    return high, (x - high.astype(F32)).astype(BF16)


def is_polar():
    lat = lax.axis_index("lat")
    return (lat == 0) | (lat == N_LAT - 1)


def polar_row(d):
    return jnp.where(lax.axis_index("lat") == N_LAT - 1, R - 1 - d, d)


def pair_select():
    row, col = iota((2 * R, R), 0), iota((2 * R, R), 1)
    return one_hot(((row >> 7) == (col >> 6)) & ((row & 127) == polar_row(col & 63)))


def pair_select_back():
    row, col = iota((R, 2 * R), 0), iota((R, 2 * R), 1)
    return one_hot(((col >> 7) == (row >> 6)) & ((col & 127) == polar_row(row & 63)))


def basis(base_ref, turn_ref):
    p = lax.axis_index("lon")
    turn = turn_ref[p]
    return base_ref[0] * turn[0:1, :] + base_ref[1] * turn[1:2, :]


def pack16(x):
    n = x.shape[0] * 8
    return jnp.concatenate([x[:, :8, :].reshape(n, R), x[:, 8:, :].reshape(n, R)], axis=1)


def spread_rows(n):
    return one_hot((iota((8 * n, n), 0) >> 3) == iota((8 * n, n), 1))


def spread_cols(n):
    return one_hot((iota((n, 8 * n), 1) >> 3) == iota((n, 8 * n), 0))


def diag8(x):
    return jnp.where((iota(x.shape, 0) & 7) == (iota(x.shape, 1) & 7), x, 0.0).astype(BF16)


def diffusion(x, zonal_weight, d, lane):
    zonal = pltpu.roll(x, 1, 0) + pltpu.roll(x, LP - 1, 0) - 2.0 * x
    east = jnp.where(lane == R - 1, 0.0, pltpu.roll(x, R - 1, 1))
    west = jnp.where(lane == 0, 0.0, pltpu.roll(x, 1, 1))
    return zonal_weight * zonal + east + west - 2.0 * x


def forward_kernel(
    table_ref, diff_ref, bias_ref, bg_ref, pert_ref, index_ref, zonal_ref, win_ref, wout_ref, base_ref, turn_ref,
    image_ref, slope_ref, spec_ref, lonmsg_ref, latmsg_ref,
    pf, bf, bias_tile, a_in, a_out,
):
    surf = jnp.zeros((L, R), F32)
    index = index_ref[...]
    for s in range(16):
        surf = jnp.where(index == s, table_ref[s], surf)
    pf[:, 0:L, :] = pert_ref[...].astype(F32)
    pf[0, 0:L, :] = pert_ref[0].astype(F32) + surf
    pf[:, L:LP, :] = jnp.zeros((C, LP - L, R), F32)
    bf[:, 0:L, :] = bg_ref[...].astype(F32)
    bf[:, L:LP, :] = jnp.zeros((C, LP - L, R), F32)
    for h in range(HID):
        bias_tile[8 * h : 8 * h + 8, :] = jnp.full((8, R), bias_ref[h], F32)

    col = iota((C, 160), 1)
    cols_in = one_hot(jnp.where(col < 144, col >> 3, 0) == iota((C, 160), 0))
    a_in[...] = diag8(dot(dot(spread_rows(HID), win_ref[...]).astype(BF16), cols_in))
    for i, part in enumerate(split(0.5 * wout_ref[...])):
        a_out[i] = diag8(dot(dot(spread_rows(C), part).astype(BF16), spread_cols(HID)))

    lane = iota((LP, R), 1)
    zonal_weight = zonal_ref[...]

    def base(c, carry):
        x = pf[c]
        d = diff_ref[c]
        image_ref[c] = x + d * diffusion(x, zonal_weight, d, lane)
        return carry

    lax.fori_loop(0, C, base, 0)

    def columns(p, carry):
        start = pl.multiple_of(p * 16, 16)
        xb = pack16(bf[:, pl.ds(start, 16), :]).astype(BF16)
        xb = jnp.concatenate([xb, jnp.zeros((16, 2 * R), BF16)], axis=0)
        pre = dot(a_in[...], xb)
        b = bias_tile[...]
        active = jnp.tanh(pre + jnp.concatenate([b, b], axis=1))
        slope = 1.0 - active * active
        slope_ref[:, pl.ds(start, 8), :] = slope[:, :R].reshape(HID, 8, R)
        slope_ref[:, pl.ds(start + 8, 8), :] = slope[:, R:].reshape(HID, 8, R)
        xp = pack16(pf[:, pl.ds(start, 16), :])
        top = xp[0:8]
        rest = top - top.astype(BF16).astype(F32)
        last = rest - rest.astype(BF16).astype(F32)
        xp = jnp.concatenate([xp, rest, last], axis=0).astype(BF16)
        high, low = split(slope * dot(a_in[...], xp))
        part = dot(a_out[0], high) + dot(a_out[0], low) + dot(a_out[1], high)
        image_ref[:, pl.ds(start, 8), :] += part[:, :R].reshape(C, 8, R)
        image_ref[:, pl.ds(start + 8, 8), :] += part[:, R:].reshape(C, 8, R)
        return carry

    lax.fori_loop(0, LP // 16, columns, 0)

    row8, lane8 = iota((8, R), 0), iota((8, R), 1)
    edge = ((lane8 == 0) & (row8 < 2)) | ((lane8 == R - 1) & (row8 >= 2) & (row8 < 4))
    pick_image = jnp.where(edge & ((row8 & 1) == 0), 1.0, 0.0)
    pick_pert = jnp.where(edge & ((row8 & 1) == 1), 1.0, 0.0)
    top = lax.Precision.HIGHEST
    for c in range(C):
        x = image_ref[c]
        lonmsg_ref[0, 0, c : c + 1, :] = x[0:1, :]
        lonmsg_ref[0, 1, c : c + 1, :] = x[LP - 1 : LP, :]
        lonmsg_ref[1, 0, c : c + 1, :] = x[L - 1 : L, :]
        lonmsg_ref[1, 1, c : c + 1, :] = x[L : L + 1, :]
        cut = dot_nt(pick_image, x, top) + dot_nt(pick_pert, diff_ref[c] * pf[c], top)
        for e in range(4):
            latmsg_ref[e // 2, e % 2, c : c + 1, 0:LP] = cut[e : e + 1, :]

    @pl.when(is_polar())
    def _():
        b = basis(base_ref, turn_ref)
        bt = jnp.concatenate([b, jnp.zeros((R - LP, R), F32)], axis=0).T
        bt_high, bt_low = split(bt[:, :LP])
        select = pair_select()
        lane64 = iota((8, R), 1) & 63

        def spectra(q, carry):
            x = jnp.concatenate([image_ref[2 * q], image_ref[2 * q + 1]], axis=1)
            high, low = split(x)
            high = dot(high, select).astype(BF16)
            low = dot(low, select).astype(BF16)
            s = dot(bt_high, high) + dot(bt_high, low) + dot(bt_low, high)
            for i, (big, small) in enumerate(FOLD):
                at = 64 * big[0] + 8 * big[1]
                tile = s[at : at + 8, :]
                if small is not None:
                    at = 64 * small[0] + 8 * small[1]
                    moved = pltpu.roll(s[at : at + 8, :], 64 - WIDTH[small[1]], 1)
                    tile = jnp.where(lane64 < WIDTH[big[1]], tile, moved)
                spec_ref[q * len(FOLD) + i] = tile
            return carry

        lax.fori_loop(0, PAIRS, spectra, 0)
        for i in range(TILES, SLOTS):
            spec_ref[i] = jnp.zeros((8, R), F32)


def exchange_kernel(
    spec_ref, lonmsg_ref, latmsg_ref, full_ref, lonrecv_ref, latrecv_ref,
    parts, total, send_sem, lon_sem, lat_sem, rs_sem, ag_sem, own_sem,
):
    lat, lon = lax.axis_index("lat"), lax.axis_index("lon")
    polar = is_polar()
    owner = lon < OWNERS
    barrier = pltpu.get_barrier_semaphore()
    left, right = lax.rem(lon + N_LON - 1, N_LON), lax.rem(lon + 1, N_LON)
    around = (left, lon, right)

    def greet(lat_to, lon_to):
        pl.semaphore_signal(barrier, inc=1, device_id=(lat_to, lon_to), device_id_type=MESH)

    @pl.when(polar & owner)
    def _():
        def tell(d, carry):
            greet(lat, lax.rem(lon + d, N_LON))
            return carry

        lax.fori_loop(1, N_LON, tell, 0)

    greet(lat, left)
    greet(lat, right)

    @pl.when(lat > 0)
    def _():
        for to in around:
            greet(lat - 1, to)

    @pl.when(lat < N_LAT - 1)
    def _():
        for to in around:
            greet(lat + 1, to)

    sides = (lat > 0).astype(jnp.int32) + (lat < N_LAT - 1).astype(jnp.int32)
    owners = polar.astype(jnp.int32) * (OWNERS - owner.astype(jnp.int32))
    pl.semaphore_wait(barrier, 2 + 3 * sides + owners)

    def remote(src, dst, send, recv, lat_to, lon_to):
        return pltpu.make_async_remote_copy(
            src_ref=src, dst_ref=dst, send_sem=send, recv_sem=recv, device_id=(lat_to, lon_to), device_id_type=MESH
        )

    def wait(ref, sem):
        pltpu.make_async_copy(ref, ref, sem).wait()

    @pl.when(polar)
    def _():
        def scatter(o, carry):
            @pl.when(o != lon)
            def _():
                remote(spec_ref.at[o], parts.at[lon], send_sem.at[0], rs_sem, lat, o).start()

            return carry

        lax.fori_loop(0, OWNERS, scatter, 0)

        @pl.when(owner)
        def _():
            pltpu.make_async_copy(spec_ref.at[lon], parts.at[lon], own_sem.at[0]).start()

    remote(lonmsg_ref.at[1], lonrecv_ref.at[0], send_sem.at[1], lon_sem, lat, right).start()
    remote(lonmsg_ref.at[0], lonrecv_ref.at[1], send_sem.at[1], lon_sem, lat, left).start()

    @pl.when(lat > 0)
    def _():
        for i, to in enumerate(around):
            remote(latmsg_ref.at[0], latrecv_ref.at[1, 2 - i], send_sem.at[2], lat_sem.at[1], lat - 1, to).start()

    @pl.when(lat < N_LAT - 1)
    def _():
        for i, to in enumerate(around):
            remote(latmsg_ref.at[1], latrecv_ref.at[0, 2 - i], send_sem.at[3], lat_sem.at[0], lat + 1, to).start()

    @pl.when(polar & owner)
    def _():
        wait(parts.at[pl.ds(0, N_LON - 1)], rs_sem)
        wait(parts.at[0], own_sem.at[0])

        def add(i, acc):
            return acc + parts[i]

        total[...] = lax.fori_loop(0, N_LON, add, jnp.zeros((PER_OWNER, 8, R), F32))

        def gather(d, carry):
            remote(total, full_ref.at[lon], send_sem.at[4], ag_sem, lat, lax.rem(lon + d, N_LON)).start()
            return carry

        lax.fori_loop(1, N_LON, gather, 0)
        pltpu.make_async_copy(total, full_ref.at[lon], own_sem.at[1]).start()
        wait(full_ref.at[pl.ds(0, OWNERS - 1)], ag_sem)
        wait(total, own_sem.at[1])
        wait(parts.at[pl.ds(0, N_LON - 1)], send_sem.at[4])
        wait(full_ref.at[pl.ds(0, OWNERS - 1)], send_sem.at[0])

    @pl.when(polar & jnp.logical_not(owner))
    def _():
        wait(full_ref, ag_sem)
        wait(full_ref, send_sem.at[0])

    wait(lonrecv_ref, lon_sem)
    wait(lonrecv_ref, send_sem.at[1])

    @pl.when(lat > 0)
    def _():
        wait(latrecv_ref.at[0], lat_sem.at[0])
        wait(latrecv_ref.at[0], send_sem.at[2])

    @pl.when(lat < N_LAT - 1)
    def _():
        wait(latrecv_ref.at[1], lat_sem.at[1])
        wait(latrecv_ref.at[1], send_sem.at[3])


def adjoint_kernel(
    diff_ref, image_ref, slope_ref, full_ref, lonrecv_ref, latrecv_ref, latmsg_ref, cutoff_ref, zonal_ref,
    win_ref, wout_ref, base_ref, turn_ref, tangent_ref, gradient_ref,
    adj, part_ref, a_back, a_in, corr,
):
    lat = lax.axis_index("lat")
    part = split(0.5 * wout_ref[...])
    col_c = spread_cols(C)
    for i in range(2):
        a_back[i] = diag8(dot(dot_nt(spread_rows(HID), part[i]).astype(BF16), col_c))
    a_in[...] = diag8(dot(dot_nt(spread_rows(C), win_ref[...]).astype(BF16), spread_cols(HID)))

    lane24 = iota((24, R), 1)
    live = iota((24, R), 0) < C

    def edge(side, own):
        image, pert = [[latrecv_ref[side, i, kind] for i in range(3)] for kind in range(2)]
        fix = jnp.where(lane24 < L, pert[1], 0.0)
        fix = jnp.where(lane24 == L, pltpu.roll(pert[2], L, 1), fix)
        fix = jnp.where(lane24 == LP - 1, pltpu.roll(pert[0], LP - L, 1), fix)
        halo = image[1] + own
        halo = halo + jnp.where(lane24 == 0, pltpu.roll(image[0], R - L, 1), 0.0)
        halo = halo + jnp.where(lane24 == L - 1, pltpu.roll(image[2], R - (LP - L), 1), 0.0)
        halo = jnp.where(lane24 < L, halo, 0.0)
        there = (lat > 0) if side == 0 else (lat < N_LAT - 1)
        return jnp.where(live & there, fix, 0.0), jnp.where(live & there, halo, 0.0)

    down_fix, down_halo = edge(0, latmsg_ref[0, 1])
    up_fix, up_halo = edge(1, latmsg_ref[1, 1])
    corr[...] = jnp.concatenate([down_fix, up_fix, down_halo, up_halo, jnp.zeros((32, R), F32)], axis=0).T

    lane = iota((LP, R), 1)
    row8 = iota((8, R), 0)

    def at_edges(c, first):
        low = corr[0:LP, first + c : first + c + 1]
        high = corr[0:LP, first + 24 + c : first + 25 + c]
        return jnp.where(lane == 0, low, jnp.where(lane == R - 1, high, 0.0))

    for c in range(C):
        adj[c] = image_ref[c] + at_edges(c, 0)
        adj[c, 0:8, :] += jnp.where(row8 == 0, lonrecv_ref[0, 1, c : c + 1, :], 0.0)
        end = jnp.where(row8 == 1, lonrecv_ref[1, 1, c : c + 1, :], 0.0)
        end = jnp.where(row8 == 2, lonrecv_ref[1, 0, c : c + 1, :], end)
        end = jnp.where(row8 == 7, lonrecv_ref[0, 0, c : c + 1, :], end)
        adj[c, LP - 8 : LP, :] += end

    @pl.when(jnp.logical_not(is_polar()))
    def _():
        tangent_ref[...] = adj[:, 0:L, :].astype(BF16)

    @pl.when(is_polar())
    def _():
        row, col = iota((R, R), 0), iota((R, R), 1)
        pick = one_hot(row == polar_row(col & 63))
        cut = dot(jnp.broadcast_to(cutoff_ref[...].astype(F32), (8, R)).astype(BF16), pick)[0:1, :]
        wave = ((row & 63) + 1).astype(F32)
        ratio = cut / wave
        g = jnp.where(wave > cut, 1.0 - ratio * ratio, 0.0)
        g_tangent = g * (2.0 / LONGITUDE_COUNT)
        g_adjoint = g_tangent * (2.0 - g)
        b_high, b_low = split(basis(base_ref, turn_ref))
        back = pair_select_back()

        def rebuild(q, carry):
            tiles = {}
            for i, (big, small) in enumerate(FOLD):
                tile = full_ref[q * len(FOLD) + i]
                tiles[big] = tile
                if small is not None:
                    tiles[small] = pltpu.roll(tile, R - 64 + WIDTH[small[1]], 1)
            s = jnp.concatenate([tiles[kind, a] for kind in (0, 1) for a in range(8)], axis=0)
            high, low = split(jnp.concatenate([g_tangent * s, g_adjoint * s], axis=1))
            removed = dot(b_high, high) + dot(b_high, low) + dot(b_low, high)
            removed = jnp.concatenate([removed[:, :R], removed[:, R:]], axis=0)
            high, low = split(removed)
            removed = dot(high, back) + dot(low, back)
            for h in range(2):
                c = 2 * q + h
                x = adj[c]
                lanes = slice(h * R, (h + 1) * R)
                tangent_ref[c] = (x - removed[:LP, lanes])[0:L].astype(BF16)
                adj[c] = x - removed[LP:, lanes]
            return carry

        lax.fori_loop(0, PAIRS, rebuild, 0)

    def columns(p, carry):
        start = pl.multiple_of(p * 16, 16)
        high, low = split(pack16(adj[:, pl.ds(start, 16), :]))
        hidden = dot(a_back[0], high) + dot(a_back[0], low) + dot(a_back[1], high)
        high, low = split(hidden * pack16(slope_ref[:, pl.ds(start, 16), :]))
        part = dot(a_in[...], high) + dot(a_in[...], low)
        part_ref[:, pl.ds(start, 8), :] = part[:, :R].reshape(C, 8, R)
        part_ref[:, pl.ds(start + 8, 8), :] = part[:, R:].reshape(C, 8, R)
        return carry

    lax.fori_loop(0, LP // 16, columns, 0)

    zonal_weight = zonal_ref[...]
    for c in range(C):
        x = adj[c]
        d = diff_ref[c]
        out = x + d * (diffusion(x, zonal_weight, d, lane) + at_edges(c, 48)) + part_ref[c]
        gradient_ref[c] = out[0:L].astype(BF16)


def vmem():
    return pl.BlockSpec(memory_space=pltpu.VMEM)


def smem():
    return pl.BlockSpec(memory_space=pltpu.SMEM)


def anywhere():
    return pl.BlockSpec(memory_space=pl.ANY)


LIMIT = 48 * 2**20


def per_device(
    background_state,
    perturbation,
    surface_pattern_index,
    surface_amplitude_table,
    cutoff,
    zonal_row_weight,
    diffusivity,
    input_weight,
    bias,
    output_weight,
):
    base, turn = (jnp.asarray(t) for t in base_tables())
    zonal = zonal_row_weight.reshape(1, R)
    message = jax.ShapeDtypeStruct((2, 2, 24, R), F32)
    image, slope, spec, lonmsg, latmsg = pl.pallas_call(
        forward_kernel,
        out_shape=(
            jax.ShapeDtypeStruct((C, LP, R), F32),
            jax.ShapeDtypeStruct((HID, LP, R), F32),
            jax.ShapeDtypeStruct((SLOTS, 8, R), F32),
            message,
            message,
        ),
        in_specs=[smem()] * 3 + [vmem()] * 8,
        out_specs=(vmem(),) * 5,
        scratch_shapes=[
            pltpu.VMEM((C, LP, R), F32),
            pltpu.VMEM((C, LP, R), F32),
            pltpu.VMEM((8 * HID, R), F32),
            pltpu.VMEM((8 * HID, 160), BF16),
            pltpu.VMEM((2, 8 * C, 8 * HID), BF16),
        ],
        compiler_params=pltpu.CompilerParams(vmem_limit_bytes=LIMIT),
        name="forward",
    )(
        surface_amplitude_table, diffusivity, bias, background_state, perturbation, surface_pattern_index, zonal,
        input_weight, output_weight, base, turn,
    )
    full, lonrecv, latrecv = pl.pallas_call(
        exchange_kernel,
        out_shape=(
            jax.ShapeDtypeStruct((OWNERS, PER_OWNER, 8, R), F32),
            message,
            jax.ShapeDtypeStruct((2, 3, 2, 24, R), F32),
        ),
        in_specs=[anywhere()] * 3,
        out_specs=(anywhere(),) * 3,
        scratch_shapes=[
            pltpu.VMEM((N_LON, PER_OWNER, 8, R), F32),
            pltpu.VMEM((PER_OWNER, 8, R), F32),
            pltpu.SemaphoreType.DMA((5,)),
            pltpu.SemaphoreType.DMA,
            pltpu.SemaphoreType.DMA((2,)),
            pltpu.SemaphoreType.DMA,
            pltpu.SemaphoreType.DMA,
            pltpu.SemaphoreType.DMA((2,)),
        ],
        compiler_params=pltpu.CompilerParams(collective_id=0, has_side_effects=True, vmem_limit_bytes=LIMIT // 4),
        name="exchange",
    )(spec.reshape(OWNERS, PER_OWNER, 8, R), lonmsg, latmsg)
    return pl.pallas_call(
        adjoint_kernel,
        out_shape=(jax.ShapeDtypeStruct((C, L, R), BF16), jax.ShapeDtypeStruct((C, L, R), BF16)),
        in_specs=[smem()] + [vmem()] * 12,
        out_specs=(vmem(), vmem()),
        scratch_shapes=[
            pltpu.VMEM((C, LP, R), F32),
            pltpu.VMEM((C, LP, R), F32),
            pltpu.VMEM((2, 8 * HID, 8 * C), BF16),
            pltpu.VMEM((8 * C, 8 * HID), BF16),
            pltpu.VMEM((R, R), F32),
        ],
        compiler_params=pltpu.CompilerParams(vmem_limit_bytes=LIMIT),
        name="adjoint",
    )(
        diffusivity, image, slope, full.reshape(SLOTS, 8, R), lonrecv, latrecv, latmsg, cutoff.reshape(1, R), zonal,
        input_weight, output_weight, base, turn,
    )


def solution(mesh):
    placed = (
        P(None, "lon", "lat"),
        P(None, "lon", "lat"),
        P("lon", "lat"),
        P(),
        P("lat"),
        P("lat"),
        P(),
        P(),
        P(),
        P(),
    )
    return jax.shard_map(
        per_device,
        mesh=mesh,
        in_specs=placed,
        out_specs=(P(None, "lon", "lat"), P(None, "lon", "lat")),
        check_vma=False,
    )
```

time: 1700 us -> 75.9 us (0.04)
  the two profiles are of different devices: /device:TPU:1 before, /device:TPU:6 now
where the time goes in v1:
time: 75.9 us; the launch traced here: 75.4 us
  Pallas kernels  64.8 us (85%)
  local copies, waits for them, and re-layouts  9.97 us (13%)
    pallas_call x1, Pallas kernels, per_device(): pl.pallas_call(exchange_kernel, out_shape=(jax.ShapeDtypeStruct((OWNERS,...  39.7 us
    pallas_call x1, Pallas kernels, per_device(): pl.pallas_call(forward_kernel, out_shape=(jax.ShapeDtypeStruct((C, LP, R)...  13.7 us
    pallas_call x1, Pallas kernels, per_device(): pl.pallas_call(adjoint_kernel, out_shape=(jax.ShapeDtypeStruct((C, L, R),...  11.4 us
    unnamed x25, local copies, waits for them, and re-layouts  9.97 us

profile of v1, /device:TPU:6, one launch (start us, length us, event | category | flops | bytes accessed | tf_op | source)
XLA Modules:
  0.0 75.4 jit_solution(93201544518150281)
XLA Ops:
  0.6 0.8 %copy.14.win_ref = bf16[48,18]{1,0:T(8,128)(2,1)S(1)} copy(bf16[48,18]{0,1:T(8,128)(2,1)} %param.19) | data formatting | bytes 3456 | tf_op args[7]
  1.4 0.0 copy-start
  1.4 1.0 %copy-done = bf16[18,90,128]{2,1,0:T(8,128)(2,1)S(1)} copy-done((bf16[18,90,128]{2,1,0:T(8,128)(2,1)S(1)}, bf16[18,90,128]{2,1,0:T(8,128)(2,1)}, u32[]{:S(2)}) %copy-start) | copy-done | bytes 414744
  2.4 0.0 copy-start.1
  2.4 1.0 %copy-done.1 = bf16[18,90,128]{2,1,0:T(8,128)(2,1)S(1)} copy-done((bf16[18,90,128]{2,1,0:T(8,128)(2,1)S(1)}, bf16[18,90,128]{2,1,0:T(8,128)(2,1)}, u32[]{:S(2)}) %copy-start.1) | copy-done | bytes 414744
  3.4 0.0 copy-start.2
  3.4 0.9 %copy-done.2 = f32[2,96,128]{2,1,0:T(8,128)S(1)} copy-done((f32[2,96,128]{2,1,0:T(8,128)S(1)}, f32[2,96,128]{2,1,0:T(8,128)}, u32[]{:S(2)}) %copy-start.2) | copy-done | bytes 98328
  4.3 0.0 copy-start.3
  4.3 0.8 %copy-done.3 = f32[64,2,128]{2,1,0:T(2,128)S(1)} copy-done((f32[64,2,128]{2,1,0:T(2,128)S(1)}, f32[64,2,128]{2,1,0:T(2,128)}, u32[]{:S(2)}) %copy-start.3) | copy-done | bytes 65560
  5.2 0.0 copy-start.4
  5.2 0.7 copy-done.4
  5.9 0.0 copy-start.5
  5.9 0.8 %copy-done.5 = s32[90,128]{1,0:T(8,128)S(1)} copy-done((s32[90,128]{1,0:T(8,128)S(1)}, s32[90,128]{1,0:T(8,128)}, u32[]{:S(2)}) %copy-start.5) | copy-done | bytes 46104
  6.7 0.0 copy-start.6
  6.7 0.7 copy-done.6
  7.3 0.0 copy-start.8
  7.3 0.7 copy-done.8
  8.0 0.0 copy-start.9
  8.0 0.7 copy-done.9
  8.7 0.0 copy-start.10
  8.7 0.7 copy-done.10
  9.3 13.7 %forward.1 = (f32[18,96,128]{2,1,0:T(8,128)S(1)}, f32[48,96,128]{2,1,0:T(8,128)S(1)}, f32[82,8,128]{2,1,0:T(8,128)S(1)}, f32[2,2,24,128]{3,2,1,0:T(8,128)S(1)}, f32[2,2,24,128]{3,2,1,0:T(8,128)S(1)}) custom-call(f32[16]{0:T(128)S(1)} %copy-done.9, f32[18]{0:T(128)S(1)} %copy-done.6, f32[48]{0:T(128)S(1)} %copy-done.10, bf16[18,90,128]{2,1,0:T(8,128)(2,1)S(1)} %copy-done, ...), custom_call_target="tpu_custom_call" | custom-call | tf_op jit(solution)/shard_map/forward/pallas_call | solution.py:476
  23.0 39.7 %exchange.1 = (f32[41,2,8,128]{3,2,1,0:T(8,128)S(1)}, f32[2,2,24,128]{3,2,1,0:T(8,128)S(1)}, f32[2,3,2,24,128]{4,3,2,1,0:T(8,128)S(1)}) custom-call(f32[41,2,8,128]{3,2,1,0:T(8,128)S(1)} %bitcast.5, f32[2,2,24,128]{3,2,1,0:T(8,128)S(1)} %get-tuple-element.13.lonmsg_ref, f32[2,2,24,128]{3,2,1,0:T(8,128)S(1)} %get-tuple-element.14.latmsg_ref), custom_call_target="tpu_custom_call" | custom-call | tf_op jit(solution)/shard_map/exchange/pallas_call | solution.py:500
  62.7 0.0 copy-start.7
  62.7 0.6 copy-done.7
  63.4 0.0 copy-start.11
  63.4 0.7 copy-done.11
  64.0 11.4 %adjoint.1 = (bf16[18,90,128]{2,1,0:T(8,128)(2,1)}, bf16[18,90,128]{2,1,0:T(8,128)(2,1)}) custom-call(f32[18]{0:T(128)S(1)} %copy-done.7, f32[18,96,128]{2,1,0:T(8,128)S(1)} %get-tuple-element.10.image_ref, f32[48,96,128]{2,1,0:T(8,128)S(1)} %get-tuple-element.11.slope_ref, f32[82,8,128]{2,1,0:T(8,128)S(1)} %bitcast.4, ...), custom_call_target="tpu_custom_call" | custom-call | tf_op jit(solution)/shard_map/adjoint/pallas_call | solution.py:522
Async XLA Ops:
  1.4 1.0 %copy-start = (bf16[18,90,128]{2,1,0:T(8,128)(2,1)S(1)}, bf16[18,90,128]{2,1,0:T(8,128)(2,1)}, u32[]{:S(2)}) copy-start(bf16[18,90,128]{2,1,0:T(8,128)(2,1)} %bg_ref.1) | copy-start | bytes 1244164
  2.4 1.0 %copy-start.1 = (bf16[18,90,128]{2,1,0:T(8,128)(2,1)S(1)}, bf16[18,90,128]{2,1,0:T(8,128)(2,1)}, u32[]{:S(2)}) copy-start(bf16[18,90,128]{2,1,0:T(8,128)(2,1)} %pert_ref.1) | copy-start | bytes 1244164
  3.4 0.9 %copy-start.2 = (f32[2,96,128]{2,1,0:T(8,128)S(1)}, f32[2,96,128]{2,1,0:T(8,128)}, u32[]{:S(2)}) copy-start(f32[2,96,128]{2,1,0:T(8,128)} %constant.4.clone.base_ref) | copy-start | bytes 294916
  4.3 0.8 %copy-start.3 = (f32[64,2,128]{2,1,0:T(2,128)S(1)}, f32[64,2,128]{2,1,0:T(2,128)}, u32[]{:S(2)}) copy-start(f32[64,2,128]{2,1,0:T(2,128)} %constant.5.clone.turn_ref) | copy-start | bytes 196612
  5.2 0.7 copy-start.4
  5.9 0.8 %copy-start.5 = (s32[90,128]{1,0:T(8,128)S(1)}, s32[90,128]{1,0:T(8,128)}, u32[]{:S(2)}) copy-start(s32[90,128]{1,0:T(8,128)} %index_ref.1) | copy-start | bytes 138244
  6.7 0.7 copy-start.6
  7.3 0.7 copy-start.8
  8.0 0.7 copy-start.9
  8.7 0.7 copy-start.10
  62.7 0.7 copy-start.7
  63.4 0.7 copy-start.11

commit v2 on v1

v2 whole, which is shorter than its diff:
```python
import functools
import math

import jax
import jax.numpy as jnp
import numpy as np
from jax import lax
from jax.experimental import pallas as pl
from jax.experimental.pallas import tpu as pltpu
from jax.sharding import PartitionSpec as P

LONGITUDE_COUNT = 5760
C = 18
HID = 48
L = 90
LP = 96
R = 128
KW = 64
N_LON = 64
N_LAT = 8
F32 = jnp.float32
BF16 = jnp.bfloat16
MESH = pl.DeviceIdType.MESH

WIDTH = [min(64, -(-(8 * a + 4) * 16 // 15)) for a in range(8)]
FOLD = []
for kind in (0, 1):
    FOLD += [((kind, 7), None), ((kind, 6), (kind, 0)), ((kind, 5), (kind, 1)), ((kind, 4), (kind, 2))]
FOLD.append(((0, 3), (1, 3)))
U_FWD, U_SPEC, U_REB, U_ADJ = 1, 3, 3, 1
PAIRS = C // 2
PER_OWNER = 3
TILES = PAIRS * len(FOLD)
OWNERS = -(-TILES // PER_OWNER)
SLOTS = OWNERS * PER_OWNER


def base_tables():
    wave = np.arange(1, KW + 1)
    rows = np.zeros((2, LP, 2 * KW), np.float64)
    for row in range(LP):
        if row <= L or row == LP - 1:
            angle = 2 * math.pi * (((row if row <= L else -1) * wave) % LONGITUDE_COUNT) / LONGITUDE_COUNT
            rows[0, row] = np.concatenate([np.cos(angle)] * 2)
            rows[1, row] = np.concatenate([np.sin(angle)] * 2)
    turn = np.zeros((N_LON, 2, 2 * KW), np.float64)
    for p in range(N_LON):
        angle = 2 * math.pi * ((p * L * wave) % LONGITUDE_COUNT) / LONGITUDE_COUNT
        turn[p, 0] = np.concatenate([np.cos(angle), np.sin(angle)])
        turn[p, 1] = np.concatenate([-np.sin(angle), np.cos(angle)])
    return rows.astype(np.float32), turn.astype(np.float32)


def iota(shape, dim):
    return lax.broadcasted_iota(jnp.int32, shape, dim)


def one_hot(mask):
    return jnp.where(mask, 1.0, 0.0).astype(BF16)


def dot(a, b):
    return lax.dot_general(a, b, (((1,), (0,)), ((), ())), preferred_element_type=F32)


def dot_nt(a, b, precision=None):
    return lax.dot_general(a, b, (((1,), (1,)), ((), ())), preferred_element_type=F32, precision=precision)


def split(x):
    high = x.astype(BF16)
    return high, (x - high.astype(F32)).astype(BF16)


def is_polar():
    lat = lax.axis_index("lat")
    return (lat == 0) | (lat == N_LAT - 1)


def polar_row(d):
    return jnp.where(lax.axis_index("lat") == N_LAT - 1, R - 1 - d, d)


def pair_select():
    row, col = iota((2 * R, R), 0), iota((2 * R, R), 1)
    return one_hot(((row >> 7) == (col >> 6)) & ((row & 127) == polar_row(col & 63)))


def pair_select_back():
    row, col = iota((R, 2 * R), 0), iota((R, 2 * R), 1)
    return one_hot(((col >> 7) == (row >> 6)) & ((col & 127) == polar_row(row & 63)))


def pack16(x):
    n = x.shape[0] * 8
    return jnp.concatenate([x[:, :8, :].reshape(n, R), x[:, 8:, :].reshape(n, R)], axis=1)


def spread_rows(n):
    return one_hot((iota((8 * n, n), 0) >> 3) == iota((8 * n, n), 1))


def spread_cols(n):
    return one_hot((iota((n, 8 * n), 1) >> 3) == iota((n, 8 * n), 0))


def diag8(x):
    return jnp.where((iota(x.shape, 0) & 7) == (iota(x.shape, 1) & 7), x, 0.0).astype(BF16)


def rows(x):
    return x.reshape(LP // 8, 8, R)


def diffusion(x, row_ref, d, lane, extra=None):
    zonal = pltpu.roll(x, 1, 0) + pltpu.roll(x, LP - 1, 0) - 2.0 * x
    east = jnp.where(lane == R - 1, 0.0, pltpu.roll(x, R - 1, 1))
    west = jnp.where(lane == 0, 0.0, pltpu.roll(x, 1, 1))
    meridional = east + west - 2.0 * x
    if extra is not None:
        meridional = meridional + extra
    return (d[None] * (row_ref[0][None] * rows(zonal) + rows(meridional))).reshape(LP, R)


def tile_of(ref, n):
    return ref[n // PER_OWNER, n % PER_OWNER]


def step_kernel(
    bg_hbm, pert_hbm, index_hbm, table_hbm, cutoff_hbm, zonal_hbm, diff_hbm, win_hbm, bias_hbm, wout_hbm, base_hbm, turn_hbm,
    tangent_ref, gradient_ref,
    image_ref, slope_ref, spec_ref, pf, d_ref, row_ref, win_ref, wout_ref, basis_ref,
    bg_ref, pert_ref, index_ref, table_ref, cutoff_ref, zonal_ref, diff_ref, bias_ref, base_ref, turn_ref,
    bf, bias_tile, a_in, a_out, mixed, sems,
    full_ref, lonrecv_ref, latrecv_ref, latmsg_ref, a_back, a_last, b_ref, back_ref, g_ref,
    parts, total, lonmsg_ref, adj, part_ref, corr, send_sem, lon_sem, lat_sem, rs_sem, ag_sem, own_sem,
):
    moves = [
        (win_hbm, win_ref), (wout_hbm, wout_ref), (bias_hbm, bias_ref), (diff_hbm, diff_ref), (table_hbm, table_ref),
        (bg_hbm, bg_ref), (pert_hbm, pert_ref), (index_hbm, index_ref), (cutoff_hbm, cutoff_ref), (zonal_hbm, zonal_ref),
        (base_hbm, base_ref), (turn_hbm.at[lax.axis_index("lon")], turn_ref),
    ]
    moves = [pltpu.make_async_copy(src, dst, sems.at[i]) for i, (src, dst) in enumerate(moves)]
    for move in moves:
        move.start()
    lat, lon = lax.axis_index("lat"), lax.axis_index("lon")
    polar = is_polar()
    owner = lon < OWNERS
    barrier = pltpu.get_barrier_semaphore()
    left, right = lax.rem(lon + N_LON - 1, N_LON), lax.rem(lon + 1, N_LON)
    around = (left, lon, right)

    def greet(lat_to, lon_to):
        pl.semaphore_signal(barrier, inc=1, device_id=(lat_to, lon_to), device_id_type=MESH)

    @pl.when(polar & owner)
    def _():
        def tell(d, carry):
            greet(lat, lax.rem(lon + d, N_LON))
            return carry

        lax.fori_loop(1, N_LON, tell, 0)

    greet(lat, left)
    greet(lat, right)

    @pl.when(lat > 0)
    def _():
        for to in around:
            greet(lat - 1, to)

    @pl.when(lat < N_LAT - 1)
    def _():
        for to in around:
            greet(lat + 1, to)

    for move in moves[:5]:
        move.wait()
    col = iota((C, 160), 1)
    cols_in = one_hot(jnp.where(col < 144, col >> 3, 0) == iota((C, 160), 0))
    a_in[...] = diag8(dot(dot_nt(spread_rows(HID), win_ref[...]).astype(BF16), cols_in))
    for i, part in enumerate(split(0.5 * wout_ref[...])):
        a_out[i] = diag8(dot(dot(spread_rows(C), part).astype(BF16), spread_cols(HID)))
    for h in range(HID):
        bias_tile[8 * h : 8 * h + 8, :] = jnp.full((8, R), bias_ref[h], F32)
    for c in range(C):
        d_ref[c] = jnp.full((8, R), diff_ref[c], F32)

    for move in moves[5:]:
        move.wait()
    surf = jnp.zeros((L, R), F32)
    index = index_ref[...]
    for s in range(16):
        surf = jnp.where(index == s, table_ref[s], surf)
    pf[:, 0:L, :] = pert_ref[...].astype(F32)
    pf[0, 0:L, :] = pert_ref[0].astype(F32) + surf
    pf[:, L:LP, :] = jnp.zeros((C, LP - L, R), F32)
    bf[:, 0:L, :] = bg_ref[...].astype(F32)
    bf[:, L:LP, :] = jnp.zeros((C, LP - L, R), F32)
    row_ref[0] = jnp.broadcast_to(zonal_ref[...], (8, R))
    row_ref[1] = jnp.broadcast_to(cutoff_ref[...].astype(F32), (8, R))
    basis_ref[...] = base_ref[0] * turn_ref[0:1, :] + base_ref[1] * turn_ref[1:2, :]

    lane = iota((LP, R), 1)

    def columns(p, carry):
        start = pl.multiple_of(p * 16, 16)
        xb = pack16(bf[:, pl.ds(start, 16), :]).astype(BF16)
        xb = jnp.concatenate([xb, jnp.zeros((16, 2 * R), BF16)], axis=0)
        pre = dot(a_in[...], xb)
        b = bias_tile[...]
        active = jnp.tanh(pre + jnp.concatenate([b, b], axis=1))
        slope = 1.0 - active * active
        slope_ref[:, pl.ds(start, 8), :] = slope[:, :R].reshape(HID, 8, R)
        slope_ref[:, pl.ds(start + 8, 8), :] = slope[:, R:].reshape(HID, 8, R)
        xp = pack16(pf[:, pl.ds(start, 16), :])
        top = xp[0:8]
        rest = top - top.astype(BF16).astype(F32)
        last = rest - rest.astype(BF16).astype(F32)
        xp = jnp.concatenate([xp, rest, last], axis=0).astype(BF16)
        high, low = split(slope * dot(a_in[...], xp))
        part = dot(a_out[0], high) + dot(a_out[0], low) + dot(a_out[1], high)
        mixed[:, pl.ds(start, 8), :] = part[:, :R].reshape(C, 8, R)
        mixed[:, pl.ds(start + 8, 8), :] = part[:, R:].reshape(C, 8, R)
        for i in range(3):
            c = 3 * p + i
            x = pf[c]
            image_ref[c] = x + diffusion(x, row_ref, d_ref[c], lane)
        return carry

    lax.fori_loop(0, LP // 16, columns, 0, unroll=U_FWD)

    @pl.when(jnp.logical_not(is_polar()))
    def _():
        image_ref[...] += mixed[...]

    @pl.when(is_polar())
    def _():
        bt = jnp.concatenate([basis_ref[...], jnp.zeros((R - LP, R), F32)], axis=0).T
        bt_high, bt_low = split(bt[:, :LP])
        select = pair_select()
        lane64 = iota((8, R), 1) & 63

        def spectra(q, carry):
            x = []
            for h in range(2):
                x.append(image_ref[2 * q + h] + mixed[2 * q + h])
                image_ref[2 * q + h] = x[h]
            high, low = split(jnp.concatenate(x, axis=1))
            high = dot(high, select).astype(BF16)
            low = dot(low, select).astype(BF16)
            s = dot(bt_high, high) + dot(bt_high, low) + dot(bt_low, high)
            for i, (big, small) in enumerate(FOLD):
                at = 64 * big[0] + 8 * big[1]
                tile = s[at : at + 8, :]
                if small is not None:
                    at = 64 * small[0] + 8 * small[1]
                    moved = pltpu.roll(s[at : at + 8, :], 64 - WIDTH[small[1]], 1)
                    tile = jnp.where(lane64 < WIDTH[big[1]], tile, moved)
                n = q * len(FOLD) + i
                spec_ref[n // PER_OWNER, n % PER_OWNER] = tile
            return carry

        lax.fori_loop(0, PAIRS, spectra, 0, unroll=U_SPEC)
        for i in range(TILES, SLOTS):
            spec_ref[i // PER_OWNER, i % PER_OWNER] = jnp.zeros((8, R), F32)

    sides = (lat > 0).astype(jnp.int32) + (lat < N_LAT - 1).astype(jnp.int32)
    owners = polar.astype(jnp.int32) * (OWNERS - owner.astype(jnp.int32))
    pl.semaphore_wait(barrier, 2 + 3 * sides + owners)

    def remote(src, dst, send, recv, lat_to, lon_to):
        return pltpu.make_async_remote_copy(
            src_ref=src, dst_ref=dst, send_sem=send, recv_sem=recv, device_id=(lat_to, lon_to), device_id_type=MESH
        )

    def wait(ref, sem):
        pltpu.make_async_copy(ref, ref, sem).wait()

    @pl.when(polar)
    def _():
        def scatter(o, carry):
            @pl.when(o != lon)
            def _():
                remote(spec_ref.at[o], parts.at[lon], send_sem.at[0], rs_sem, lat, o).start()

            return carry

        lax.fori_loop(0, OWNERS, scatter, 0)

        @pl.when(owner)
        def _():
            pltpu.make_async_copy(spec_ref.at[lon], parts.at[lon], own_sem.at[0]).start()

    row8, lane8 = iota((8, R), 0), iota((8, R), 1)
    edge = ((lane8 == 0) & (row8 < 2)) | ((lane8 == R - 1) & (row8 >= 2) & (row8 < 4))
    pick_image = jnp.where(edge & ((row8 & 1) == 0), 1.0, 0.0)
    pick_pert = jnp.where(edge & ((row8 & 1) == 1), 1.0, 0.0)
    top = lax.Precision.HIGHEST
    for c in range(C):
        x = image_ref[c]
        lonmsg_ref[0, 0, c : c + 1, :] = x[0:1, :]
        lonmsg_ref[0, 1, c : c + 1, :] = x[LP - 1 : LP, :]
        lonmsg_ref[1, 0, c : c + 1, :] = x[L - 1 : L, :]
        lonmsg_ref[1, 1, c : c + 1, :] = x[L : L + 1, :]
        cut = dot_nt(pick_image, x, top) + dot_nt(pick_pert, (d_ref[c][None] * rows(pf[c])).reshape(LP, R), top)
        for e in range(4):
            latmsg_ref[e // 2, e % 2, c : c + 1, 0:LP] = cut[e : e + 1, :]

    remote(lonmsg_ref.at[1], lonrecv_ref.at[0], send_sem.at[1], lon_sem, lat, right).start()
    remote(lonmsg_ref.at[0], lonrecv_ref.at[1], send_sem.at[1], lon_sem, lat, left).start()

    @pl.when(lat > 0)
    def _():
        for i, to in enumerate(around):
            remote(latmsg_ref.at[0], latrecv_ref.at[1, 2 - i], send_sem.at[2], lat_sem.at[1], lat - 1, to).start()

    @pl.when(lat < N_LAT - 1)
    def _():
        for i, to in enumerate(around):
            remote(latmsg_ref.at[1], latrecv_ref.at[0, 2 - i], send_sem.at[3], lat_sem.at[0], lat + 1, to).start()

    part = split(0.5 * wout_ref[...])
    col_c = spread_cols(C)
    for i in range(2):
        a_back[i] = diag8(dot(dot_nt(spread_rows(HID), part[i]).astype(BF16), col_c))
    a_last[...] = diag8(dot(dot(spread_rows(C), win_ref[...]).astype(BF16), spread_cols(HID)))

    @pl.when(polar)
    def _():
        row, col = iota((R, R), 0), iota((R, R), 1)
        pick = one_hot(row == polar_row(col & 63))
        cut = dot(row_ref[1].astype(BF16), pick)[0:1, :]
        wave = ((row & 63) + 1).astype(F32)
        ratio = cut / wave
        g = jnp.where(wave > cut, 1.0 - ratio * ratio, 0.0)
        g_ref[0] = g * (2.0 / LONGITUDE_COUNT)
        g_ref[1] = g * (2.0 - g) * (2.0 / LONGITUDE_COUNT)
        b_ref[0], b_ref[1] = split(basis_ref[...])
        back_ref[...] = pair_select_back()

    @pl.when(polar & owner)
    def _():
        wait(parts.at[pl.ds(0, N_LON - 1)], rs_sem)
        wait(parts.at[0], own_sem.at[0])

        def add(i, acc):
            return acc + parts[i]

        total[...] = lax.fori_loop(0, N_LON, add, jnp.zeros((PER_OWNER, 8, R), F32))

        def gather(d, carry):
            remote(total, full_ref.at[lon], send_sem.at[4], ag_sem, lat, lax.rem(lon + d, N_LON)).start()
            return carry

        lax.fori_loop(1, N_LON, gather, 0)
        pltpu.make_async_copy(total, full_ref.at[lon], own_sem.at[1]).start()

    wait(lonrecv_ref, lon_sem)
    wait(lonrecv_ref, send_sem.at[1])

    @pl.when(lat > 0)
    def _():
        wait(latrecv_ref.at[0], lat_sem.at[0])
        wait(latrecv_ref.at[0], send_sem.at[2])

    @pl.when(lat < N_LAT - 1)
    def _():
        wait(latrecv_ref.at[1], lat_sem.at[1])
        wait(latrecv_ref.at[1], send_sem.at[3])

    lane24 = iota((24, R), 1)
    live = iota((24, R), 0) < C

    def neighbours(side, own):
        image, pert = [[latrecv_ref[side, i, kind] for i in range(3)] for kind in range(2)]
        fix = jnp.where(lane24 < L, pert[1], 0.0)
        fix = jnp.where(lane24 == L, pltpu.roll(pert[2], L, 1), fix)
        fix = jnp.where(lane24 == LP - 1, pltpu.roll(pert[0], LP - L, 1), fix)
        halo = image[1] + own
        halo = halo + jnp.where(lane24 == 0, pltpu.roll(image[0], R - L, 1), 0.0)
        halo = halo + jnp.where(lane24 == L - 1, pltpu.roll(image[2], R - (LP - L), 1), 0.0)
        halo = jnp.where(lane24 < L, halo, 0.0)
        there = (lat > 0) if side == 0 else (lat < N_LAT - 1)
        return jnp.where(live & there, fix, 0.0), jnp.where(live & there, halo, 0.0)

    down_fix, down_halo = neighbours(0, latmsg_ref[0, 1])
    up_fix, up_halo = neighbours(1, latmsg_ref[1, 1])
    corr[...] = jnp.concatenate([down_fix, up_fix, down_halo, up_halo, jnp.zeros((32, R), F32)], axis=0).T

    lane = iota((LP, R), 1)
    row8 = iota((8, R), 0)

    def at_edges(c, first):
        low = corr[0:LP, first + c : first + c + 1]
        high = corr[0:LP, first + 24 + c : first + 25 + c]
        return jnp.where(lane == 0, low, jnp.where(lane == R - 1, high, 0.0))

    for c in range(C):
        adj[c] = image_ref[c] + at_edges(c, 0)
        adj[c, 0:8, :] += jnp.where(row8 == 0, lonrecv_ref[0, 1, c : c + 1, :], 0.0)
        end = jnp.where(row8 == 1, lonrecv_ref[1, 1, c : c + 1, :], 0.0)
        end = jnp.where(row8 == 2, lonrecv_ref[1, 0, c : c + 1, :], end)
        end = jnp.where(row8 == 7, lonrecv_ref[0, 0, c : c + 1, :], end)
        adj[c, LP - 8 : LP, :] += end

    @pl.when(polar & owner)
    def _():
        wait(full_ref.at[pl.ds(0, OWNERS - 1)], ag_sem)
        wait(total, own_sem.at[1])
        wait(parts.at[pl.ds(0, N_LON - 1)], send_sem.at[4])
        wait(full_ref.at[pl.ds(0, OWNERS - 1)], send_sem.at[0])

    @pl.when(polar & jnp.logical_not(owner))
    def _():
        wait(full_ref, ag_sem)
        wait(full_ref, send_sem.at[0])

    @pl.when(jnp.logical_not(is_polar()))
    def _():
        tangent_ref[...] = adj[:, 0:L, :].astype(BF16)

    @pl.when(is_polar())
    def _():
        g_tangent, g_adjoint = g_ref[0], g_ref[1]
        b_high, b_low = b_ref[0], b_ref[1]
        back = back_ref[...]

        def rebuild(q, carry):
            tiles = {}
            for i, (big, small) in enumerate(FOLD):
                tile = tile_of(full_ref, q * len(FOLD) + i)
                tiles[big] = tile
                if small is not None:
                    tiles[small] = pltpu.roll(tile, R - 64 + WIDTH[small[1]], 1)
            s = jnp.concatenate([tiles[kind, a] for kind in (0, 1) for a in range(8)], axis=0)
            high, low = split(jnp.concatenate([g_tangent * s, g_adjoint * s], axis=1))
            removed = dot(b_high, high) + dot(b_high, low) + dot(b_low, high)
            removed = jnp.concatenate([removed[:, :R], removed[:, R:]], axis=0)
            high, low = split(removed)
            removed = dot(high, back) + dot(low, back)
            for h in range(2):
                c = 2 * q + h
                x = adj[c]
                lanes = slice(h * R, (h + 1) * R)
                tangent_ref[c] = (x - removed[:LP, lanes])[0:L].astype(BF16)
                adj[c] = x - removed[LP:, lanes]
            return carry

        lax.fori_loop(0, PAIRS, rebuild, 0, unroll=U_REB)

    def columns_back(p, carry):
        start = pl.multiple_of(p * 16, 16)
        high, low = split(pack16(adj[:, pl.ds(start, 16), :]))
        hidden = dot(a_back[0], high) + dot(a_back[0], low) + dot(a_back[1], high)
        high, low = split(hidden * pack16(slope_ref[:, pl.ds(start, 16), :]))
        part = dot(a_last[...], high) + dot(a_last[...], low)
        part_ref[:, pl.ds(start, 8), :] = part[:, :R].reshape(C, 8, R)
        part_ref[:, pl.ds(start + 8, 8), :] = part[:, R:].reshape(C, 8, R)
        return carry

    lax.fori_loop(0, LP // 16, columns_back, 0, unroll=U_ADJ)

    for c in range(C):
        x = adj[c]
        out = x + diffusion(x, row_ref, d_ref[c], lane, at_edges(c, 48)) + part_ref[c]
        gradient_ref[c] = out[0:L].astype(BF16)


def vmem():
    return pl.BlockSpec(memory_space=pltpu.VMEM)


def hbm():
    return pl.BlockSpec(memory_space=pltpu.HBM)


def anywhere():
    return pl.BlockSpec(memory_space=pl.ANY)


LIMIT = 58 * 2**20


def per_device(
    background_state,
    perturbation,
    surface_pattern_index,
    surface_amplitude_table,
    cutoff,
    zonal_row_weight,
    diffusivity,
    input_weight,
    bias,
    output_weight,
):
    base, turn = (jnp.asarray(t) for t in base_tables())
    shape = jax.ShapeDtypeStruct
    scratch = pltpu.VMEM
    field = scratch((C, LP, R), F32)
    message = scratch((2, 2, 24, R), F32)
    dma = pltpu.SemaphoreType.DMA
    return pl.pallas_call(
        step_kernel,
        out_shape=(shape((C, L, R), BF16), shape((C, L, R), BF16)),
        in_specs=[hbm()] * 12,
        out_specs=(vmem(), vmem()),
        scratch_shapes=[
            field,
            scratch((HID, LP, R), F32),
            scratch((OWNERS, PER_OWNER, 8, R), F32),
            field,
            scratch((C, 8, R), F32),
            scratch((2, 8, R), F32),
            scratch((C, HID), BF16),
            scratch((C, HID), F32),
            scratch((LP, R), F32),
            scratch((C, L, R), BF16),
            scratch((C, L, R), BF16),
            scratch((L, R), jnp.int32),
            pltpu.SMEM((16,), F32),
            scratch((1, R), jnp.int32),
            scratch((1, R), F32),
            pltpu.SMEM((C,), F32),
            pltpu.SMEM((HID,), F32),
            scratch((2, LP, R), F32),
            scratch((2, R), F32),
            field,
            scratch((8 * HID, R), F32),
            scratch((8 * HID, 160), BF16),
            scratch((2, 8 * C, 8 * HID), BF16),
            field,
            dma((12,)),
            scratch((OWNERS, PER_OWNER, 8, R), F32),
            message,
            scratch((2, 3, 2, 24, R), F32),
            message,
            scratch((2, 8 * HID, 8 * C), BF16),
            scratch((8 * C, 8 * HID), BF16),
            scratch((2, LP, R), BF16),
            scratch((R, 2 * R), BF16),
            scratch((2, R, R), F32),
            scratch((N_LON, PER_OWNER, 8, R), F32),
            scratch((PER_OWNER, 8, R), F32),
            message,
            field,
            field,
            scratch((R, R), F32),
            dma((5,)),
            dma,
            dma((2,)),
            dma,
            dma,
            dma((2,)),
        ],
        compiler_params=pltpu.CompilerParams(collective_id=0, has_side_effects=True, vmem_limit_bytes=LIMIT),
        name="step",
    )(
        background_state, perturbation, surface_pattern_index, surface_amplitude_table, cutoff.reshape(1, R),
        zonal_row_weight.reshape(1, R), diffusivity, input_weight.T, bias, output_weight, base, turn,
    )


def solution(mesh):
    placed = (
        P(None, "lon", "lat"),
        P(None, "lon", "lat"),
        P("lon", "lat"),
        P(),
        P("lat"),
        P("lat"),
        P(),
        P(),
        P(),
        P(),
    )
    return jax.shard_map(
        per_device,
        mesh=mesh,
        in_specs=placed,
        out_specs=(P(None, "lon", "lat"), P(None, "lon", "lat")),
        check_vma=False,
    )
```

time: 75.9 us -> 51.7 us (0.68)
  the two profiles are of different devices: /device:TPU:6 before, /device:TPU:48 now
where the time goes in v2:
time: 51.7 us; the launch traced here: 51.6 us
  Pallas kernels  48.3 us (93%)
  local copies, waits for them, and re-layouts  2.62 us (5%)
  between operations  0.65 us (1%)
    pallas_call x1, Pallas kernels, per_device(): pl.pallas_call(step_kernel, out_shape=(shape((C, L, R), BF16), shape((C,...  48.3 us
    unnamed x4, local copies, waits for them, and re-layouts  2.62 us

profile of v2, /device:TPU:48, one launch (start us, length us, event | category | flops | bytes accessed | tf_op | source)
XLA Modules:
  0.0 51.6 jit_solution(16309395476861254223)
XLA Ops:
  0.6 48.3 %step.1 = (bf16[18,90,128]{2,1,0:T(8,128)(2,1)}, bf16[18,90,128]{2,1,0:T(8,128)(2,1)}) custom-call(bf16[18,90,128]{2,1,0:T(8,128)(2,1)} %bg_hbm.1, bf16[18,90,128]{2,1,0:T(8,128)(2,1)} %pert_hbm.1, s32[90,128]{1,0:T(8,128)} %index_hbm.1, f32[16]{0:T(128)} %table_hbm.1, s32[1,128]{1,0:T(1,128)} %bitcast.4, f32[1,128]{1,0:T(1,128)} %bitcast.5, f32[18]{0:T(128)} %diff_hbm.1, ...), custom_call_target="tpu_custom_call" | custom-call | tf_op jit(solution)/shard_map/step/pallas_call | solution.py:503
  48.9 0.0 copy-start
  48.9 1.9 %copy.16 = bf16[18,90,128]{2,1,0:T(8,128)(2,1)} copy(bf16[18,90,128]{2,1,0:T(8,128)(2,1)} %get-tuple-element.4) | data formatting | bytes 829440
  50.8 0.0 copy-done
  50.8 0.8 %copy.17 = bf16[18,90,128]{2,1,0:T(8,128)(2,1)} copy(bf16[18,90,128]{2,1,0:T(8,128)(2,1)S(1)} %copy-done) | data formatting | bytes 829440
Async XLA Ops:
  48.9 1.9 %copy-start = (bf16[18,90,128]{2,1,0:T(8,128)(2,1)S(1)}, bf16[18,90,128]{2,1,0:T(8,128)(2,1)}, u32[]{:S(2)}) copy-start(bf16[18,90,128]{2,1,0:T(8,128)(2,1)} %get-tuple-element.5) | copy-start | bytes 1244164

commit v3 on v2

--- a/solution.py
+++ b/solution.py
@@ -18,6 +18,7 @@
 KW = 64
 N_LON = 64
 N_LAT = 8
+PLANE = 32
 F32 = jnp.float32
 BF16 = jnp.bfloat16
 MESH = pl.DeviceIdType.MESH
@@ -27,7 +28,7 @@
 for kind in (0, 1):
     FOLD += [((kind, 7), None), ((kind, 6), (kind, 0)), ((kind, 5), (kind, 1)), ((kind, 4), (kind, 2))]
 FOLD.append(((0, 3), (1, 3)))
-U_FWD, U_SPEC, U_REB, U_ADJ = 1, 3, 3, 1
+U_FWD, U_SPEC, U_REB, U_ADJ = 3, 9, 9, 6
 PAIRS = C // 2
 PER_OWNER = 3
 TILES = PAIRS * len(FOLD)
@@ -133,7 +134,7 @@
     bg_ref, pert_ref, index_ref, table_ref, cutoff_ref, zonal_ref, diff_ref, bias_ref, base_ref, turn_ref,
     bf, bias_tile, a_in, a_out, mixed, sems,
     full_ref, lonrecv_ref, latrecv_ref, latmsg_ref, a_back, a_last, b_ref, back_ref, g_ref,
-    parts, total, lonmsg_ref, adj, part_ref, corr, send_sem, lon_sem, lat_sem, rs_sem, ag_sem, own_sem,
+    parts, total, lonmsg_ref, adj, part_ref, corr, send_sem, lon_sem, lat_sem, rs_sem, ag_sem, own_sem, pair_sem,
 ):
     moves = [
         (win_hbm, win_ref), (wout_hbm, wout_ref), (bias_hbm, bias_ref), (diff_hbm, diff_ref), (table_hbm, table_ref),
@@ -145,7 +146,10 @@
         move.start()
     lat, lon = lax.axis_index("lat"), lax.axis_index("lon")
     polar = is_polar()
-    owner = lon < OWNERS
+    here = lax.rem(lon, PLANE)
+    first = lon - here
+    owner = here < OWNERS
+    partner = lax.rem(lon + PLANE, N_LON)
     barrier = pltpu.get_barrier_semaphore()
     left, right = lax.rem(lon + N_LON - 1, N_LON), lax.rem(lon + 1, N_LON)
     around = (left, lon, right)
@@ -156,10 +160,11 @@
     @pl.when(polar & owner)
     def _():
         def tell(d, carry):
-            greet(lat, lax.rem(lon + d, N_LON))
+            greet(lat, first + lax.rem(here + d, PLANE))
             return carry
 
-        lax.fori_loop(1, N_LON, tell, 0)
+        lax.fori_loop(1, PLANE, tell, 0)
+        greet(lat, partner)
 
     greet(lat, left)
     greet(lat, right)
@@ -266,7 +271,7 @@
             spec_ref[i // PER_OWNER, i % PER_OWNER] = jnp.zeros((8, R), F32)
 
     sides = (lat > 0).astype(jnp.int32) + (lat < N_LAT - 1).astype(jnp.int32)
-    owners = polar.astype(jnp.int32) * (OWNERS - owner.astype(jnp.int32))
+    owners = polar.astype(jnp.int32) * OWNERS
     pl.semaphore_wait(barrier, 2 + 3 * sides + owners)
 
     def remote(src, dst, send, recv, lat_to, lon_to):
@@ -280,9 +285,9 @@
     @pl.when(polar)
     def _():
         def scatter(o, carry):
-            @pl.when(o != lon)
+            @pl.when(o != here)
             def _():
-                remote(spec_ref.at[o], parts.at[lon], send_sem.at[0], rs_sem, lat, o).start()
+                remote(spec_ref.at[o], parts.at[here], send_sem.at[0], rs_sem, lat, first + o).start()
 
             return carry
 
@@ -290,7 +295,7 @@
 
         @pl.when(owner)
         def _():
-            pltpu.make_async_copy(spec_ref.at[lon], parts.at[lon], own_sem.at[0]).start()
+            pltpu.make_async_copy(spec_ref.at[here], parts.at[here], own_sem.at[0]).start()
 
     row8, lane8 = iota((8, R), 0), iota((8, R), 1)
     edge = ((lane8 == 0) & (row8 < 2)) | ((lane8 == R - 1) & (row8 >= 2) & (row8 < 4))
@@ -341,20 +346,24 @@
 
     @pl.when(polar & owner)
     def _():
-        wait(parts.at[pl.ds(0, N_LON - 1)], rs_sem)
+        wait(parts.at[pl.ds(0, PLANE - 1)], rs_sem)
         wait(parts.at[0], own_sem.at[0])
 
         def add(i, acc):
             return acc + parts[i]
 
-        total[...] = lax.fori_loop(0, N_LON, add, jnp.zeros((PER_OWNER, 8, R), F32))
+        total[0] = lax.fori_loop(1, PLANE, add, parts[0], unroll=True)
+        remote(total.at[0], total.at[1], send_sem.at[5], pair_sem, lat, partner).start()
+        wait(total.at[1], pair_sem)
+        total[2] = total[0] + total[1]
 
         def gather(d, carry):
-            remote(total, full_ref.at[lon], send_sem.at[4], ag_sem, lat, lax.rem(lon + d, N_LON)).start()
+            to = first + lax.rem(here + d, PLANE)
+            remote(total.at[2], full_ref.at[here], send_sem.at[4], ag_sem, lat, to).start()
             return carry
 
-        lax.fori_loop(1, N_LON, gather, 0)
-        pltpu.make_async_copy(total, full_ref.at[lon], own_sem.at[1]).start()
+        lax.fori_loop(1, PLANE, gather, 0)
+        pltpu.make_async_copy(total.at[2], full_ref.at[here], own_sem.at[1]).start()
 
     wait(lonrecv_ref, lon_sem)
     wait(lonrecv_ref, send_sem.at[1])
@@ -407,8 +416,9 @@
     @pl.when(polar & owner)
     def _():
         wait(full_ref.at[pl.ds(0, OWNERS - 1)], ag_sem)
-        wait(total, own_sem.at[1])
-        wait(parts.at[pl.ds(0, N_LON - 1)], send_sem.at[4])
+        wait(total.at[2], own_sem.at[1])
+        wait(total.at[0], send_sem.at[5])
+        wait(parts.at[pl.ds(0, PLANE - 1)], send_sem.at[4])
         wait(full_ref.at[pl.ds(0, OWNERS - 1)], send_sem.at[0])
 
     @pl.when(polar & jnp.logical_not(owner))
@@ -540,18 +550,19 @@
             scratch((2, LP, R), BF16),
             scratch((R, 2 * R), BF16),
             scratch((2, R, R), F32),
-            scratch((N_LON, PER_OWNER, 8, R), F32),
-            scratch((PER_OWNER, 8, R), F32),
+            scratch((PLANE, PER_OWNER, 8, R), F32),
+            scratch((3, PER_OWNER, 8, R), F32),
             message,
             field,
             field,
             scratch((R, R), F32),
-            dma((5,)),
+            dma((6,)),
             dma,
             dma((2,)),
             dma,
             dma,
             dma((2,)),
+            dma,
         ],
         compiler_params=pltpu.CompilerParams(collective_id=0, has_side_effects=True, vmem_limit_bytes=LIMIT),
         name="step",

time: 51.7 us -> 45.2 us (0.87)
  the two profiles are of different devices: /device:TPU:48 before, /device:TPU:2 now
where the time goes in v3:
time: 45.2 us; the launch traced here: 45.1 us
  Pallas kernels  41.8 us (92%)
  local copies, waits for them, and re-layouts  2.62 us (6%)
  between operations  0.65 us (1%)
    pallas_call x1, Pallas kernels, per_device(): pl.pallas_call(step_kernel, out_shape=(shape((C, L, R), BF16), shape((C,...  41.8 us
    unnamed x4, local copies, waits for them, and re-layouts  2.62 us

profile of v3, /device:TPU:2, one launch (start us, length us, event | category | flops | bytes accessed | tf_op | source)
XLA Modules:
  0.0 45.1 jit_solution(3345184170384573781)
XLA Ops:
  0.6 41.8 %step.1 = (bf16[18,90,128]{2,1,0:T(8,128)(2,1)}, bf16[18,90,128]{2,1,0:T(8,128)(2,1)}) custom-call(bf16[18,90,128]{2,1,0:T(8,128)(2,1)} %bg_hbm.1, bf16[18,90,128]{2,1,0:T(8,128)(2,1)} %pert_hbm.1, s32[90,128]{1,0:T(8,128)} %index_hbm.1, f32[16]{0:T(128)} %table_hbm.1, s32[1,128]{1,0:T(1,128)} %bitcast.4, f32[1,128]{1,0:T(1,128)} %bitcast.5, f32[18]{0:T(128)} %diff_hbm.1, ...), custom_call_target="tpu_custom_call" | custom-call | tf_op jit(solution)/shard_map/step/pallas_call | solution.py:513
  42.4 0.0 copy-start
  42.4 1.9 %copy.16 = bf16[18,90,128]{2,1,0:T(8,128)(2,1)} copy(bf16[18,90,128]{2,1,0:T(8,128)(2,1)} %get-tuple-element.4) | data formatting | bytes 829440
  44.3 0.0 copy-done
  44.3 0.8 %copy.17 = bf16[18,90,128]{2,1,0:T(8,128)(2,1)} copy(bf16[18,90,128]{2,1,0:T(8,128)(2,1)S(1)} %copy-done) | data formatting | bytes 829440
Async XLA Ops:
  42.4 1.9 %copy-start = (bf16[18,90,128]{2,1,0:T(8,128)(2,1)S(1)}, bf16[18,90,128]{2,1,0:T(8,128)(2,1)}, u32[]{:S(2)}) copy-start(bf16[18,90,128]{2,1,0:T(8,128)(2,1)} %get-tuple-element.5) | copy-start | bytes 1244164

commit v4 on v3

--- a/solution.py
+++ b/solution.py
@@ -28,7 +28,7 @@
 for kind in (0, 1):
     FOLD += [((kind, 7), None), ((kind, 6), (kind, 0)), ((kind, 5), (kind, 1)), ((kind, 4), (kind, 2))]
 FOLD.append(((0, 3), (1, 3)))
-U_FWD, U_SPEC, U_REB, U_ADJ = 3, 9, 9, 6
+U_FWD, U_SPEC, U_REB, U_ADJ = 3, 9, 9, 3
 PAIRS = C // 2
 PER_OWNER = 3
 TILES = PAIRS * len(FOLD)
@@ -129,7 +129,8 @@
 
 def step_kernel(
     bg_hbm, pert_hbm, index_hbm, table_hbm, cutoff_hbm, zonal_hbm, diff_hbm, win_hbm, bias_hbm, wout_hbm, base_hbm, turn_hbm,
-    tangent_ref, gradient_ref,
+    tangent_hbm, gradient_hbm,
+    tangent_ref, gradient_ref, out_sems,
     image_ref, slope_ref, spec_ref, pf, d_ref, row_ref, win_ref, wout_ref, basis_ref,
     bg_ref, pert_ref, index_ref, table_ref, cutoff_ref, zonal_ref, diff_ref, bias_ref, base_ref, turn_ref,
     bf, bias_tile, a_in, a_out, mixed, sems,
@@ -413,6 +414,38 @@
         end = jnp.where(row8 == 7, lonrecv_ref[0, 0, c : c + 1, :], end)
         adj[c, LP - 8 : LP, :] += end
 
+    polar_half = (lat == N_LAT - 1).astype(jnp.int32)
+
+    def half_columns(half, first):
+        at_low, at_high = half * 64, (1 - half) * 64
+
+        def two(x, y):
+            mask = lax.broadcasted_iota(jnp.int32, x.shape, x.ndim - 1) < 64
+            return jnp.where(mask, pltpu.roll(x, at_low, x.ndim - 1), pltpu.roll(y, at_high, y.ndim - 1))
+
+        def packed(ref, n, start):
+            t = [ref[:, pl.ds(start + 8 * j, 8), :].reshape(8 * n, R) for j in range(4)]
+            return jnp.concatenate([two(t[0], t[1]), two(t[2], t[3])], axis=1)
+
+        def body(p, carry):
+            start = pl.multiple_of(p * 32, 32)
+            high, low = split(packed(adj, C, start))
+            hidden = dot(a_back[0], high) + dot(a_back[0], low) + dot(a_back[1], high)
+            high, low = split(hidden * packed(slope_ref, HID, start))
+            out = dot(a_last[...], high) + dot(a_last[...], low)
+            for j in range(4):
+                tile = pltpu.roll(out[:, (j // 2) * R : (j // 2 + 1) * R], at_high if j % 2 else at_low, 1).reshape(C, 8, R)
+                rows8 = pl.ds(start + 8 * j, 8)
+                if not first:
+                    mask = (lax.broadcasted_iota(jnp.int32, (C, 8, R), 2) >> 6) == half
+                    tile = jnp.where(mask, tile, part_ref[:, rows8, :])
+                part_ref[:, rows8, :] = tile
+            return carry
+
+        lax.fori_loop(0, LP // 32, body, 0, unroll=U_ADJ)
+
+    half_columns(1 - polar_half, True)
+
     @pl.when(polar & owner)
     def _():
         wait(full_ref.at[pl.ds(0, OWNERS - 1)], ag_sem)
@@ -459,26 +492,37 @@
 
         lax.fori_loop(0, PAIRS, rebuild, 0, unroll=U_REB)
 
-    def columns_back(p, carry):
-        start = pl.multiple_of(p * 16, 16)
-        high, low = split(pack16(adj[:, pl.ds(start, 16), :]))
-        hidden = dot(a_back[0], high) + dot(a_back[0], low) + dot(a_back[1], high)
-        high, low = split(hidden * pack16(slope_ref[:, pl.ds(start, 16), :]))
-        part = dot(a_last[...], high) + dot(a_last[...], low)
-        part_ref[:, pl.ds(start, 8), :] = part[:, :R].reshape(C, 8, R)
-        part_ref[:, pl.ds(start + 8, 8), :] = part[:, R:].reshape(C, 8, R)
-        return carry
-
-    lax.fori_loop(0, LP // 16, columns_back, 0, unroll=U_ADJ)
+    tangent_out = pltpu.make_async_copy(tangent_ref, tangent_hbm, out_sems.at[0])
+    tangent_out.start()
+
+    half_columns(polar_half, False)
+    outs = [tangent_out]
 
     for c in range(C):
         x = adj[c]
         out = x + diffusion(x, row_ref, d_ref[c], lane, at_edges(c, 48)) + part_ref[c]
         gradient_ref[c] = out[0:L].astype(BF16)
-
-
-def vmem():
-    return pl.BlockSpec(memory_space=pltpu.VMEM)
+        if c % 6 == 5:
+            part = pl.ds(c - 5, 6)
+            outs.append(pltpu.make_async_copy(gradient_ref.at[part], gradient_hbm.at[part], out_sems.at[1 + c // 6]))
+            outs[-1].start()
+    for move in outs:
+        move.wait()
+
+
+def settle_kernel(tangent_ref, gradient_ref, tangent_out, gradient_out, held, sems):
+    ends = ((tangent_ref, tangent_out), (gradient_ref, gradient_out))
+    half = C // 2
+    parts = [(i, pl.ds(h * half, half)) for i in range(2) for h in range(2)]
+    loads = [pltpu.make_async_copy(ends[i][0].at[p], held.at[i, p], sems.at[0, n]) for n, (i, p) in enumerate(parts)]
+    stores = [pltpu.make_async_copy(held.at[i, p], ends[i][1].at[p], sems.at[1, n]) for n, (i, p) in enumerate(parts)]
+    for load in loads:
+        load.start()
+    for load, store in zip(loads, stores):
+        load.wait()
+        store.start()
+    for store in stores:
+        store.wait()
 
 
 def hbm():
@@ -510,12 +554,15 @@
     field = scratch((C, LP, R), F32)
     message = scratch((2, 2, 24, R), F32)
     dma = pltpu.SemaphoreType.DMA
-    return pl.pallas_call(
+    tangent, gradient = pl.pallas_call(
         step_kernel,
         out_shape=(shape((C, L, R), BF16), shape((C, L, R), BF16)),
         in_specs=[hbm()] * 12,
-        out_specs=(vmem(), vmem()),
+        out_specs=(hbm(), hbm()),
         scratch_shapes=[
+            scratch((C, L, R), BF16),
+            scratch((C, L, R), BF16),
+            dma((4,)),
             field,
             scratch((HID, LP, R), F32),
             scratch((OWNERS, PER_OWNER, 8, R), F32),
@@ -570,6 +617,15 @@
         background_state, perturbation, surface_pattern_index, surface_amplitude_table, cutoff.reshape(1, R),
         zonal_row_weight.reshape(1, R), diffusivity, input_weight.T, bias, output_weight, base, turn,
     )
+    return pl.pallas_call(
+        settle_kernel,
+        out_shape=(shape((C, L, R), BF16), shape((C, L, R), BF16)),
+        in_specs=[hbm()] * 2,
+        out_specs=(hbm(), hbm()),
+        scratch_shapes=[scratch((2, C, L, R), BF16), dma((2, 4))],
+        compiler_params=pltpu.CompilerParams(vmem_limit_bytes=LIMIT),
+        name="settle",
+    )(tangent, gradient)
 
 
 def solution(mesh):

time: 45.2 us -> 43.5 us (0.962)
  local copies, waits for them, and re-layouts: 2.62 us -> 0 us
  Pallas kernels: 41.8 us -> 42.7 us
    unnamed x4 -> x0, local copies, waits for them, and re-layouts: 2.62 us -> none
    pallas_call x0 -> x1, Pallas kernels: none -> 2.02 us  [per_device(): pl.pallas_call(settle_kernel, out_shape=(shape((C, L, R), BF16), shape((C...]
    pallas_call x1, Pallas kernels: 41.8 us -> 40.6 us  [per_device(): pl.pallas_call(step_kernel, out_shape=(shape((C, L, R), BF16), shape((C,...]
where the time goes in v4:
time: 43.5 us; the launch traced here: 43.3 us
  Pallas kernels  42.7 us (98%)
  between operations  0.64 us (1%)
    pallas_call x1, Pallas kernels, per_device(): pl.pallas_call(step_kernel, out_shape=(shape((C, L, R), BF16), shape((C,...  40.6 us
    pallas_call x1, Pallas kernels, per_device(): pl.pallas_call(settle_kernel, out_shape=(shape((C, L, R), BF16), shape((C...  2.02 us

profile of v4, /device:TPU:2, one launch (start us, length us, event | category | flops | bytes accessed | tf_op | source)
XLA Modules:
  0.0 43.3 jit_solution(4639819782831672204)
XLA Ops:
  0.6 40.6 %step.1 = (bf16[18,90,128]{2,1,0:T(8,128)(2,1)}, bf16[18,90,128]{2,1,0:T(8,128)(2,1)}) custom-call(bf16[18,90,128]{2,1,0:T(8,128)(2,1)} %bg_hbm.1, bf16[18,90,128]{2,1,0:T(8,128)(2,1)} %pert_hbm.1, s32[90,128]{1,0:T(8,128)} %index_hbm.1, f32[16]{0:T(128)} %table_hbm.1, s32[1,128]{1,0:T(1,128)} %bitcast.4, f32[1,128]{1,0:T(1,128)} %bitcast.5, f32[18]{0:T(128)} %diff_hbm.1, ...), custom_call_target="tpu_custom_call" | custom-call | tf_op jit(solution)/shard_map/step/pallas_call | solution.py:557
  41.3 2.0 %settle.1 = (bf16[18,90,128]{2,1,0:T(8,128)(2,1)}, bf16[18,90,128]{2,1,0:T(8,128)(2,1)}) custom-call(bf16[18,90,128]{2,1,0:T(8,128)(2,1)} %get-tuple-element.4.tangent_ref, bf16[18,90,128]{2,1,0:T(8,128)(2,1)} %get-tuple-element.5.gradient_ref), custom_call_target="tpu_custom_call" | custom-call | tf_op jit(solution)/shard_map/settle/pallas_call | solution.py:620
